TPU v7x, 32 devices: a whole 2x2x4 slice. The times are simulated.
32 devices in a mesh: dom: 8 (over z, y), rep: 4 (over x, core).
Axes of the slice: x: 2, y: 2, z: 4, core: 2. Of those that a mesh axis runs over, the one named last changes fastest.
Arguments:
- profiles: bfloat16 [300, 8192], P(None, 'dom'), may hold values from -6 to 6
- pack_index: int32 [8, 4, 8, 16], P('dom', 'rep'), may hold values from 0 to 1023, as said below
- obs_slot: int32 [4, 16384], P(None, ('dom', 'rep')), may hold values from 0 to 127, as said below
- interp_weight: float32 [4, 16384], P(None, ('dom', 'rep')), may hold values from 0 to 1, as said below
- departures: float32 [100, 16384], P(None, ('dom', 'rep')), may hold values from -6 to 6
- w_in: bfloat16 [300, 512], replicated, may hold values from -0.375 to 0.375
- b_in: float32 [512], replicated, may hold values from -4 to 4
- w_mid: bfloat16 [512, 512], replicated, may hold values from -0.25 to 0.25
- b_mid: float32 [512], replicated, may hold values from -4 to 4
- w_out: bfloat16 [512, 100], replicated, may hold values from -0.25 to 0.25
Outputs:
- column_adjoint: float32 [300, 8192], P(None, ('dom', 'rep'))
Inputs may be any that keep to these rules, and one draw needn't show every extreme that they name: Local column numbers within the partition that holds pack_index's first index; the 16 columns of pack_index[o, r, d, :] are distinct and lie in quarter d % 4 of the partition, that is from (d % 4) * 256 to one less than (d % 4 + 1) * 256. `obs_slot`: slot o * 16 + j names the j-th column that the observation's segment and replica index take from partition o; where o lies more than 2 partitions from the segment's own index, counted cyclically, j < 4. `interp_weight`: bilinear weights: the four of an observation sum to one.
All inputs are finite; a program needn't handle non-finite values.
Results may differ from a plain program's by a relative error of at most 0.0057.
Values may be sent and summed in bfloat16 or wider, within the bound.
A program may use at most 64 MiB of HBM per device.

v0:
```python
import jax
import jax.numpy as jnp
from jax import lax
from jax.sharding import PartitionSpec as P


def contract_first(matrix, values):
    return lax.dot_general(
        matrix, values, (((0,), (0,)), ((), ())), preferred_element_type=jnp.float32
    )


def interpolate(fetched, obs_slot, interp_weight):
    summed = jnp.zeros((fetched.shape[0], obs_slot.shape[1]), jnp.float32)
    for corner in range(4):
        summed = summed + interp_weight[corner] * jnp.take(
            fetched, obs_slot[corner], axis=1
        ).astype(jnp.float32)
    return summed.astype(jnp.bfloat16)


def network_adjoint(inputs, departures, w_in, b_in, w_mid, b_mid, w_out):
    z_one = contract_first(w_in, inputs) + b_in[:, None]
    act_one = jnp.tanh(z_one).astype(jnp.bfloat16)
    z_two = contract_first(w_mid, act_one) + b_mid[:, None]
    cot_out = departures.astype(jnp.bfloat16)
    g_two = (
        jnp.dot(w_out, cot_out, preferred_element_type=jnp.float32) * (1.0 - jnp.tanh(z_two) ** 2)
    ).astype(jnp.bfloat16)
    g_one = (
        jnp.dot(w_mid, g_two, preferred_element_type=jnp.float32) * (1.0 - jnp.tanh(z_one) ** 2)
    ).astype(jnp.bfloat16)
    return jnp.dot(w_in, g_one, preferred_element_type=jnp.float32)


def spread_slots(g_inputs, obs_slot, interp_weight, slot_total):
    slot_adjoint = jnp.zeros((g_inputs.shape[0], slot_total), jnp.float32)
    for corner in range(4):
        slot_adjoint = slot_adjoint.at[:, obs_slot[corner]].add(interp_weight[corner] * g_inputs)
    return slot_adjoint


def route_rows(values, columns, quarter):
    feature_count = values.shape[0]
    rep_count = lax.axis_size("rep")
    seg_count, per_seg = columns.shape
    grouped = (
        values.reshape(feature_count, seg_count // rep_count, rep_count, per_seg)
        .transpose(0, 2, 1, 3)
        .reshape(feature_count, seg_count * per_seg)
    )
    grouped_cols = (
        columns.reshape(seg_count // rep_count, rep_count, per_seg)
        .transpose(1, 0, 2)
        .reshape(1, seg_count * per_seg)
    )
    received, received_cols = (
        lax.all_to_all(grouped, "rep", split_axis=1, concat_axis=1, tiled=True),
        lax.all_to_all(grouped_cols, "rep", split_axis=1, concat_axis=1, tiled=True),
    )
    local_cols = received_cols[0] - lax.axis_index("rep") * quarter
    return jnp.zeros((feature_count, quarter), jnp.float32).at[:, local_cols].add(received)


def body(
    profiles, pack_index, obs_slot, interp_weight, departures, w_in, b_in, w_mid, b_mid, w_out
):
    send_lists = pack_index[0, 0]
    quarter = profiles.shape[1] // lax.axis_size("rep")
    packed = jnp.take(profiles, send_lists.reshape(-1), axis=1)
    fetched = lax.all_to_all(packed, "dom", split_axis=1, concat_axis=1, tiled=True)
    inputs = interpolate(fetched, obs_slot, interp_weight)
    g_inputs = network_adjoint(inputs, departures, w_in, b_in, w_mid, b_mid, w_out)
    slot_adjoint = spread_slots(g_inputs, obs_slot, interp_weight, fetched.shape[1])
    main_values = lax.all_to_all(slot_adjoint, "dom", split_axis=1, concat_axis=1, tiled=True)
    share = route_rows(main_values, send_lists, quarter)
    return share


def solution(mesh):
    placed = (
        P(None, "dom"),
        P("dom", "rep", None, None),
        P(None, ("dom", "rep")),
        P(None, ("dom", "rep")),
        P(None, ("dom", "rep")),
        P(),
        P(),
        P(),
        P(),
        P(),
    )
    return jax.shard_map(
        body, mesh=mesh, in_specs=placed, out_specs=P(None, ("dom", "rep")), check_vma=False
    )
```

profile of v0, /device:TPU:1, one launch (start us, length us, event | category | flops | bytes accessed | tf_op | source)
XLA Modules:
  0.0 84.8 jit_solution(1270457005312143867)
XLA Ops:
  0.0 0.0 copy-start
  0.0 0.0 copy-start.6
  0.0 0.8 reshape_squeeze.10
  0.8 0.0 copy-done.6
  0.9 1.4 %copy.29 = bf16[300,1024]{0,1:T(8,128)(2,1)S(1)} copy(bf16[300,1024]{1,0:T(8,128)(2,1)} %param.12) | data formatting | bytes 1228800 | tf_op args[0]
  2.3 0.9 %gather_fusion = bf16[128,300]{1,0:T(8,128)(2,1)S(1)} fusion(bf16[300,1024]{0,1:T(8,128)(2,1)S(1)} %copy.29, s32[1024]{0:T(1024)S(1)} %pad_clamp_fusion.4), kind=kCustom, calls=%fused_computation.4 | custom fusion | bytes 154112 | tf_op jit(solution)/shard_map/jit(_take)/gather | solution.py:70
  3.2 0.0 copy-start.4
  3.2 0.7 broadcast_select_fusion
  3.9 6.5 %all-to-all-start.1 = ((bf16[300,8,16]{0,2,1:T(8,128)(2,1)}), bf16[300,8,16]{0,2,1:T(8,128)(2,1)S(1)}, u32[]{:S(2)}, u32[]{:S(2)}) async-start(bf16[300,8,16]{0,2,1:T(8,128)(2,1)} %broadcast_select_fusion), calls=%async_computation.1 | async-start | bytes 196608 | tf_op jit(solution)/shard_map/all_to_all | solution.py:71
  10.4 0.0 copy-done.7
  10.6 0.0 copy-start.8
  10.6 0.7 copy-done.8
  11.3 0.0 copy-done.4
  11.3 0.0 copy-done.5
  11.3 0.3 fusion.32
  11.6 0.7 all_to_all.26
  12.3 4.2 %all-to-all-done.1 = bf16[300,8,16]{0,2,1:T(8,128)(2,1)S(1)} async-done(((bf16[300,8,16]{0,2,1:T(8,128)(2,1)}), bf16[300,8,16]{0,2,1:T(8,128)(2,1)S(1)}, u32[]{:S(2)}, u32[]{:S(2)}) %all-to-all-start.1) | async-done | bytes 76832 | tf_op jit(solution)/shard_map/all_to_all | solution.py:71
  16.5 5.2 %all-to-all-start = ((s32[1,4,32]{2,0,1:T(1,128)}), s32[1,4,32]{2,0,1:T(1,128)S(1)}, u32[]{:S(2)}, u32[]{:S(2)}) async-start(s32[1,4,32]{2,0,1:T(1,128)} %bitcast.2), calls=%async_computation | async-start | bytes 4096 | tf_op jit(solution)/shard_map/all_to_all | solution.py:59
  21.7 1.9 %gather_fusion.1 = bf16[512,300]{1,0:T(8,128)(2,1)S(1)} fusion(bf16[300,128]{0,1:T(8,128)(2,1)S(1)} %bitcast.78, s32[1024]{0:T(1024)S(1)} %pad_clamp_fusion.3), kind=kCustom, calls=%fused_computation.clone | custom fusion | bytes 616448 | tf_op jit(solution)/shard_map/jit(_take)/gather | solution.py:16
  23.7 2.6 %gather_fusion.2 = bf16[512,300]{1,0:T(8,128)(2,1)} fusion(bf16[300,128]{0,1:T(8,128)(2,1)S(1)} %bitcast.79, s32[1024]{0:T(1024)S(1)} %pad_clamp_fusion.2), kind=kCustom, calls=%fused_computation.1.clone | custom fusion | bytes 616448 | tf_op jit(solution)/shard_map/jit(_take)/gather | solution.py:16
  26.2 2.6 %gather_fusion.3 = bf16[512,300]{1,0:T(8,128)(2,1)} fusion(bf16[300,128]{0,1:T(8,128)(2,1)S(1)} %bitcast.80, s32[1024]{0:T(1024)S(1)} %pad_clamp_fusion.1), kind=kCustom, calls=%fused_computation.2.clone | custom fusion | bytes 616448 | tf_op jit(solution)/shard_map/jit(_take)/gather | solution.py:16
  28.8 2.6 %gather_fusion.4 = bf16[512,300]{1,0:T(8,128)(2,1)} fusion(bf16[300,128]{0,1:T(8,128)(2,1)S(1)} %bitcast.81, s32[1024]{0:T(1024)S(1)} %pad_clamp_fusion), kind=kCustom, calls=%fused_computation.3.clone | custom fusion | bytes 616448 | tf_op jit(solution)/shard_map/jit(_take)/gather | solution.py:16
  31.4 0.0 copy-done.3
  31.4 0.7 copy-done.10
  32.0 2.4 %fusion.5 = f32[512,512]{0,1:T(8,128)S(1)} fusion(bf16[300,512]{1,0:T(8,128)(2,1)S(1)} %copy-done.3, f32[512]{0:T(512)S(1)} %copy-done.10, bf16[512,300]{1,0:T(8,128)(2,1)} %gather_fusion.4, bf16[512,300]{1,0:T(8,128)(2,1)} %gather_fusion.3, bf16[512,300]{1,0:T(8,128)(2,1)} %gather_fusion.2, bf16[512,300]{1,0:T(8,128)(2,1)S(1)} %gather_fusion.1, ...), kind=kOutput, calls=%fused_computation.18 | convolution fusion | flops 160006144 | bytes 2596864 | tf_op jit(solution)/shard_map/dot_general | solution.py:8
  34.4 0.0 copy-done
  34.4 0.0 copy-done.9
  34.4 1.3 %fusion.6 = bf16[512,512]{1,0:T(8,128)(2,1)} fusion(f32[512,512]{1,0:T(8,128)S(1)} %fusion.32, bf16[512,512]{1,0:T(8,128)(2,1)S(1)} %copy-done, f32[512]{0:T(512)S(1)} %copy-done.9, f32[512,512]{0,1:T(8,128)S(1)} %fusion.5), kind=kOutput, calls=%fused_computation.19 | convolution fusion | flops 270008320 | bytes 3147776 | tf_op jit(solution)/shard_map/dot_general | solution.py:8
  35.8 3.0 %broadcast_multiply_fusion = (f32[512,300]{0,1:T(8,128)S(1)}, f32[512,300]{0,1:T(8,128)}, f32[512,300]{0,1:T(8,128)}, f32[512,300]{0,1:T(8,128)S(1)}) fusion(f32[512]{0:T(512)S(1)} %bitcast.99, f32[512]{0:T(512)S(1)} %bitcast.101, f32[512]{0:T(512)S(1)} %bitcast.97, f32[512]{0:T(512)S(1)} %bitcast.95, bf16[300,512]{1,0:T(8,128)(2,1)} %param.17, ...), kind=kOutput, calls=%fused_computation.43 | convolution fusion | flops 427384832 | bytes 4870144 | tf_op jit(solution)/shard_map/dot_general | solution.py:33
  38.7 1.1 %copy.33 = f32[512,300]{1,0:T(8,128)} copy(f32[512,300]{0,1:T(8,128)S(1)} %get-tuple-element.9) | data formatting | bytes 1228800 | tf_op jit(solution)/shard_map/mul | solution.py:39
  39.9 0.0 copy-done.2
  39.9 0.3 copy.34
  40.2 0.8 copy-done.1
  41.0 0.3 copy.35
  41.2 0.3 copy.36
  41.5 4.8 %scatter_custom_fusion = f32[300,128]{0,1:T(8,128)} fusion(s32[512]{0:T(512)S(1)} %bitcast.105, f32[512,300]{1,0:T(8,128)} %copy.33, f32[]{:T(128)} %constant.8.clone.1), kind=kCustom, calls=%fused_computation.52 | custom fusion | flops 153600 | bytes 154112 | tf_op jit(solution)/shard_map/scatter-add | solution.py:39
  46.3 5.1 %scatter_fusion = f32[300,128]{0,1:T(8,128)} fusion(f32[300,128]{0,1:T(8,128)} %scatter_custom_fusion, s32[512]{0:T(512)S(1)} %bitcast.104, f32[512,300]{1,0:T(8,128)S(1)} %copy.34), kind=kCustom, calls=%fused_computation.6 | custom fusion | flops 153600 | bytes 1845248 | tf_op jit(solution)/shard_map/scatter-add | solution.py:39
  51.4 5.1 %scatter_fusion.1 = f32[300,128]{0,1:T(8,128)} fusion(f32[300,128]{0,1:T(8,128)} %scatter_fusion, s32[512]{0:T(512)S(1)} %bitcast.103, f32[512,300]{1,0:T(8,128)S(1)} %copy.35), kind=kCustom, calls=%fused_computation.7 | custom fusion | flops 153600 | bytes 1845248 | tf_op jit(solution)/shard_map/scatter-add | solution.py:39
  56.6 5.1 %scatter_fusion.2 = f32[300,128]{0,1:T(8,128)} fusion(f32[300,128]{0,1:T(8,128)} %scatter_fusion.1, s32[512]{0:T(512)S(1)} %bitcast.102, f32[512,300]{1,0:T(8,128)S(1)} %copy.36), kind=kCustom, calls=%fused_computation.8 | custom fusion | flops 153600 | bytes 1845248 | tf_op jit(solution)/shard_map/scatter-add | solution.py:39
  61.7 0.0 all-to-all-done
  61.7 3.4 %all-to-all-start.2 = ((f32[300,8,16]{0,2,1:T(8,128)}), f32[300,8,16]{0,2,1:T(8,128)S(1)}, u32[]{:S(2)}, u32[]{:S(2)}) async-start(f32[300,8,16]{0,2,1:T(8,128)} %bitcast.30), calls=%async_computation.2 | async-start | bytes 393216 | tf_op jit(solution)/shard_map/all_to_all | solution.py:75
  65.1 0.1 sub.30
  65.2 7.3 %all-to-all-done.2 = f32[300,8,16]{0,2,1:T(8,128)S(1)} async-done(((f32[300,8,16]{0,2,1:T(8,128)}), f32[300,8,16]{0,2,1:T(8,128)S(1)}, u32[]{:S(2)}, u32[]{:S(2)}) %all-to-all-start.2) | async-done | bytes 153632 | tf_op jit(solution)/shard_map/all_to_all | solution.py:75
  72.6 0.7 copy.37
  73.2 4.7 %all-to-all-start.3 = ((f32[300,4,32]{0,2,1:T(8,128)}), f32[300,4,32]{0,2,1:T(8,128)S(1)}, u32[]{:S(2)}, u32[]{:S(2)}) async-start(f32[300,4,32]{0,2,1:T(8,128)} %bitcast.33), calls=%async_computation.3 | async-start | bytes 393216 | tf_op jit(solution)/shard_map/all_to_all | solution.py:58
  78.0 4.5 %all-to-all-done.3 = f32[300,4,32]{0,2,1:T(8,128)S(1)} async-done(((f32[300,4,32]{0,2,1:T(8,128)}), f32[300,4,32]{0,2,1:T(8,128)S(1)}, u32[]{:S(2)}, u32[]{:S(2)}) %all-to-all-start.3) | async-done | bytes 153632 | tf_op jit(solution)/shard_map/all_to_all | solution.py:58
  82.4 1.4 %scatter_custom_fusion.4 = f32[300,256]{0,1:T(8,128)S(1)} fusion(s32[128]{0:T(128)S(1)} %fusion.36, f32[128,300]{1,0:T(8,128)S(1)} %bitcast.84, f32[]{:T(128)} %constant.8.clone.1), kind=kCustom, calls=%fused_computation.48 | custom fusion | flops 38400 | bytes 307204 | tf_op jit(solution)/shard_map/scatter-add | solution.py:62
  83.9 0.9 %copy.38 = f32[300,256]{1,0:T(8,128)} copy(f32[300,256]{0,1:T(8,128)S(1)} %scatter_custom_fusion.4) | data formatting | bytes 614400 | tf_op jit(solution)/shard_map/scatter-add | solution.py:62
  (26 shorter events, 0.1 us)
Async XLA Ops:
  0.0 34.4 %copy-start = (bf16[512,512]{1,0:T(8,128)(2,1)S(1)}, bf16[512,512]{1,0:T(8,128)(2,1)}, u32[]{:S(2)}) copy-start(bf16[512,512]{1,0:T(8,128)(2,1)} %param.19) | copy-start | bytes 1572868
  0.0 0.8 copy-start.6
  3.2 8.1 %copy-start.4 = (f32[100,512]{1,0:T(8,128)S(1)}, f32[100,512]{1,0:T(8,128)}, u32[]{:S(2)}) copy-start(f32[100,512]{1,0:T(8,128)} %param.16) | copy-start | bytes 614404
  3.9 6.5 %copy-start.7 = (s32[4,512]{1,0:T(4,128)S(1)}, s32[4,512]{1,0:T(4,128)}, u32[]{:S(2)}) copy-start(s32[4,512]{1,0:T(4,128)} %param.14) | copy-start | bytes 24580
  3.9 7.4 %copy-start.5 = (bf16[512,100]{0,1:T(8,128)(2,1)S(1)}, bf16[512,100]{0,1:T(8,128)(2,1)}, u32[]{:S(2)}) copy-start(bf16[512,100]{0,1:T(8,128)(2,1)} %param.21) | copy-start | bytes 307204
  3.9 12.6 %all-to-all-start.1 = ((bf16[300,8,16]{0,2,1:T(8,128)(2,1)}), bf16[300,8,16]{0,2,1:T(8,128)(2,1)S(1)}, u32[]{:S(2)}, u32[]{:S(2)}) async-start(bf16[300,8,16]{0,2,1:T(8,128)(2,1)} %broadcast_select_fusion), calls=%async_computation.1 | async-start | bytes 196608 | tf_op jit(solution)/shard_map/all_to_all | solution.py:71
  10.6 0.7 copy-start.8
  16.5 45.2 %all-to-all-start = ((s32[1,4,32]{2,0,1:T(1,128)}), s32[1,4,32]{2,0,1:T(1,128)S(1)}, u32[]{:S(2)}, u32[]{:S(2)}) async-start(s32[1,4,32]{2,0,1:T(1,128)} %bitcast.2), calls=%async_computation | async-start | bytes 4096 | tf_op jit(solution)/shard_map/all_to_all | solution.py:59
  28.8 2.6 %copy-start.3 = (bf16[300,512]{1,0:T(8,128)(2,1)S(1)}, bf16[300,512]{1,0:T(8,128)(2,1)}, u32[]{:S(2)}) copy-start(bf16[300,512]{1,0:T(8,128)(2,1)} %param.17) | copy-start | bytes 921604
  31.4 0.7 copy-start.10
  32.0 2.4 %copy-start.9 = (f32[512]{0:T(512)S(1)}, f32[512]{0:T(512)}, u32[]{:S(2)}) copy-start(f32[512]{0:T(512)} %param.20) | copy-start | bytes 6148
  38.7 1.2 %copy-start.2 = (f32[512,300]{0,1:T(8,128)S(1)}, f32[512,300]{0,1:T(8,128)}, u32[]{:S(2)}) copy-start(f32[512,300]{0,1:T(8,128)} %get-tuple-element.8) | copy-start | bytes 1843204
  39.9 1.1 %copy-start.1 = (f32[512,300]{0,1:T(8,128)S(1)}, f32[512,300]{0,1:T(8,128)}, u32[]{:S(2)}) copy-start(f32[512,300]{0,1:T(8,128)} %get-tuple-element.7) | copy-start | bytes 1843204
  61.7 10.8 %all-to-all-start.2 = ((f32[300,8,16]{0,2,1:T(8,128)}), f32[300,8,16]{0,2,1:T(8,128)S(1)}, u32[]{:S(2)}, u32[]{:S(2)}) async-start(f32[300,8,16]{0,2,1:T(8,128)} %bitcast.30), calls=%async_computation.2 | async-start | bytes 393216 | tf_op jit(solution)/shard_map/all_to_all | solution.py:75
  73.2 9.2 %all-to-all-start.3 = ((f32[300,4,32]{0,2,1:T(8,128)}), f32[300,4,32]{0,2,1:T(8,128)S(1)}, u32[]{:S(2)}, u32[]{:S(2)}) async-start(f32[300,4,32]{0,2,1:T(8,128)} %bitcast.33), calls=%async_computation.3 | async-start | bytes 393216 | tf_op jit(solution)/shard_map/all_to_all | solution.py:58
where the time goes:
time: 86.3 us; the launch traced here: 84.8 us
  other arithmetic  22.5 us (26%)
  starting transfers between devices  19.8 us (23%)
  local copies, waits for them, and re-layouts  19.2 us (22%)
  waiting for transfers between devices  16 us (19%)
  matrix products  6.99 us (8%)
    scatter-add x4, other arithmetic, spread_slots(): slot_adjoint.at[:, obs_slot[corner]].add(interp_weight[corner] * g_inputs)  20.2 us
    gather x4, local copies, waits for them, and re-layouts, interpolate(): jnp.take(fetched, obs_slot[corner], axis=1).astype(jnp.float32)  9.63 us
    all_to_all x1, waiting for transfers between devices, body(): lax.all_to_all(slot_adjoint, 'dom', split_axis=1, concat_axis=1, tiled=True)  7.33 us
    all_to_all x1, starting transfers between devices, body(): lax.all_to_all(packed, 'dom', split_axis=1, concat_axis=1, tiled=True)  6.51 us
    all_to_all x1, starting transfers between devices, route_rows(): lax.all_to_all(grouped_cols, 'rep', split_axis=1, concat_axis=1, tiled=True)  5.19 us
    all_to_all x1, starting transfers between devices, route_rows(): lax.all_to_all(grouped, 'rep', split_axis=1, concat_axis=1, tiled=True)  4.73 us
    all_to_all x1, waiting for transfers between devices, route_rows(): lax.all_to_all(grouped, 'rep', split_axis=1, concat_axis=1, tiled=True)  4.46 us
    all_to_all x1, waiting for transfers between devices, body(): lax.all_to_all(packed, 'dom', split_axis=1, concat_axis=1, tiled=True)  4.22 us
  transfers between devices with their start and end apart: 4, of which 3 were waited for; matrix products, arithmetic and copies ran while one was open for 46% of the time, Pallas kernels for 0%

commit v1 on v0

v1 whole, which is shorter than its diff:
```python
import functools

import jax
import jax.numpy as jnp
from jax import lax
from jax.experimental import pallas as pl
from jax.experimental.pallas import tpu as pltpu
from jax.sharding import PartitionSpec as P

MESH = pl.DeviceIdType.MESH
F32 = jnp.float32
BF16 = jnp.bfloat16


def dot_nn(a, b):
    return lax.dot_general(a, b, (((1,), (0,)), ((), ())), preferred_element_type=F32)


def dot_nt(a, b):
    return lax.dot_general(a, b, (((1,), (1,)), ((), ())), preferred_element_type=F32)


def dot_tn(a, b):
    return lax.dot_general(a, b, (((0,), (0,)), ((), ())), preferred_element_type=F32)


def split_high_low(x):
    high = x.astype(BF16)
    return high, (x - high.astype(F32)).astype(BF16)


def pick_column(pick, table, cap):
    rows = pick.shape[0]
    spread = dot_nn(pick, table)
    lane = lax.broadcasted_iota(jnp.int32, (rows, cap), 1)
    row = lax.broadcasted_iota(jnp.int32, (rows, cap), 0)
    return jnp.sum(jnp.where(lane == row % cap, spread, 0.0), axis=1, keepdims=True)


def kernel(
    n_dom,
    n_rep,
    profiles_ref,
    pack_ref,
    slot_ref,
    weight_ref,
    departures_hbm,
    w_in_hbm,
    b_in_ref,
    w_mid_hbm,
    b_mid_ref,
    w_out_hbm,
    out_ref,
    departures_ref,
    w_in_ref,
    w_mid_ref,
    w_out_ref,
    send_fwd,
    fetched,
    index_all,
    spread_t,
    spread_s,
    g_out,
    send_bwd,
    returned,
    load_sem,
    idx_send,
    idx_recv,
    fwd_send,
    fwd_recv,
    bwd_send,
    bwd_recv,
):
    dom, rep = lax.axis_index("dom"), lax.axis_index("rep")
    cap = pack_ref.shape[1]
    per_rep = n_dom // n_rep
    slots = n_dom * cap
    feats = profiles_ref.shape[0]
    obs = slot_ref.shape[1]
    quarter = profiles_ref.shape[1] // n_rep
    my_part, my_group = dom % n_rep, dom // n_rep

    barrier = pltpu.get_barrier_semaphore()
    for step in range(1, n_rep):
        pl.semaphore_signal(
            barrier, inc=1, device_id=(dom, (rep + step) % n_rep), device_id_type=MESH
        )

    def greet(step, carry):
        pl.semaphore_signal(
            barrier, inc=1, device_id=((dom + step) % n_dom, rep), device_id_type=MESH
        )
        return carry

    lax.fori_loop(1, n_dom, greet, 0, unroll=n_dom <= 16)

    loads = [
        pltpu.make_async_copy(source, target, load_sem.at[k])
        for k, (source, target) in enumerate(
            (
                (departures_hbm, departures_ref),
                (w_out_hbm, w_out_ref),
                (w_in_hbm, w_in_ref),
                (w_mid_hbm, w_mid_ref),
            )
        )
    ]
    for load in loads:
        load.start()

    seg = lax.broadcasted_iota(jnp.int32, (n_dom, cap), 0)
    local = pack_ref[...] - (seg % n_rep) * quarter
    index_all[rep] = local
    row = lax.broadcasted_iota(jnp.int32, (slots, n_dom), 0) // cap
    col = lax.broadcasted_iota(jnp.int32, (slots, n_dom), 1)
    pick = (col == (row % per_rep) * n_rep + row // per_rep).astype(BF16)
    column = pick_column(pick, local.astype(BF16), cap).astype(jnp.int32)
    part_rows = per_rep * cap
    for part in range(n_rep):
        hot = (
            column[part * part_rows : (part + 1) * part_rows]
            == lax.broadcasted_iota(jnp.int32, (part_rows, quarter), 1)
        ).astype(BF16)
        packed = dot_nt(hot, profiles_ref[:, part * quarter : (part + 1) * quarter])
        send_fwd[part] = packed.astype(BF16).reshape(per_rep, cap, feats)

    pl.semaphore_wait(barrier, n_dom + n_rep - 2)

    def fwd_copy(step):
        peer = (dom + step) % n_dom
        return pltpu.make_async_remote_copy(
            src_ref=send_fwd.at[peer % n_rep, peer // n_rep],
            dst_ref=fetched.at[dom],
            send_sem=fwd_send.at[step],
            recv_sem=fwd_recv.at[step],
            device_id=(peer, rep),
            device_id_type=MESH,
        )

    def fwd_start(step, carry):
        fwd_copy(step).start()
        return carry

    lax.fori_loop(1, n_dom, fwd_start, 0, unroll=n_dom <= 16)

    idx_copies = [
        pltpu.make_async_remote_copy(
            src_ref=index_all.at[rep],
            dst_ref=index_all.at[rep],
            send_sem=idx_send.at[step],
            recv_sem=idx_recv.at[step],
            device_id=(dom, (rep + step) % n_rep),
            device_id_type=MESH,
        )
        for step in range(1, n_rep)
    ]
    for copy in idx_copies:
        copy.start()

    fetched[dom] = send_fwd[my_part, my_group]

    chunk = 128 if slots % 128 == 0 else slots

    def build(c, carry):
        first = pl.multiple_of(c * chunk, chunk)
        ids = lax.broadcasted_iota(jnp.int32, (chunk, obs), 0) + first
        total = jnp.zeros((chunk, obs), F32)
        for k in range(4):
            total = total + jnp.where(ids == slot_ref[k : k + 1, :], weight_ref[k : k + 1, :], 0.0)
        high, low = split_high_low(total)
        spread_s[0, pl.ds(first, chunk), :] = high
        spread_s[1, pl.ds(first, chunk), :] = low
        high_t, low_t = split_high_low(total.T)
        spread_t[:, pl.ds(first, chunk)] = high_t
        spread_t[:, pl.ds(pl.multiple_of(slots + first, chunk), chunk)] = low_t
        return carry

    lax.fori_loop(0, slots // chunk, build, 0, unroll=slots == chunk)

    loads[0].wait()
    loads[1].wait()
    g_out[...] = dot_nt(departures_ref[...].T.astype(BF16), w_out_ref[...])
    loads[2].wait()
    loads[3].wait()

    def fwd_wait(step, carry):
        fwd_copy(step).wait()
        return carry

    lax.fori_loop(1, n_dom, fwd_wait, 0, unroll=n_dom <= 16)

    columns = fetched[...].reshape(slots, feats)
    inputs = dot_nn(spread_t[...], jnp.concatenate([columns, columns], axis=0)).astype(BF16)
    act_one = jnp.tanh(dot_nn(inputs, w_in_ref[...]) + b_in_ref[...])
    act_two = jnp.tanh(dot_nn(act_one.astype(BF16), w_mid_ref[...]) + b_mid_ref[...])
    g_two = (g_out[...] * (1.0 - act_two * act_two)).astype(BF16)
    g_one = (dot_nt(g_two, w_mid_ref[...]) * (1.0 - act_one * act_one)).astype(BF16)
    hidden = dot_nn(spread_s[0], g_one) + dot_nn(spread_s[1], g_one)
    slot_adjoint = dot_nt(hidden.astype(BF16), w_in_ref[...])
    send_bwd[...] = slot_adjoint.astype(BF16).reshape(n_dom, cap, feats)

    def bwd_copy(step):
        owner = (dom + step) % n_dom
        return pltpu.make_async_remote_copy(
            src_ref=send_bwd.at[owner],
            dst_ref=returned.at[my_group * n_rep + rep],
            send_sem=bwd_send.at[step],
            recv_sem=bwd_recv.at[my_group * n_rep + rep],
            device_id=(owner, my_part),
            device_id_type=MESH,
        )

    def bwd_start(step, carry):
        bwd_copy(step).start()
        return carry

    lax.fori_loop(1, n_dom, bwd_start, 0, unroll=n_dom <= 16)

    @pl.when(my_part != rep)
    def _():
        bwd_copy(0).start()

    @pl.when(my_part == rep)
    def _():
        returned[my_group * n_rep + rep] = send_bwd[dom]

    for copy in idx_copies:
        copy.wait()
    table = index_all[...].astype(BF16).reshape(n_rep * n_dom, cap)
    row = lax.broadcasted_iota(jnp.int32, (slots, n_rep * n_dom), 0) // cap
    col = lax.broadcasted_iota(jnp.int32, (slots, n_rep * n_dom), 1)
    pick = (col == (row % n_rep) * n_dom + (row // n_rep) * n_rep + rep).astype(BF16)
    target = pick_column(pick, table, cap).astype(jnp.int32)
    hot = (target == lax.broadcasted_iota(jnp.int32, (slots, quarter), 1)).astype(BF16)

    def bwd_wait(sender, carry):
        from_dom = (sender // n_rep) * n_rep + rep
        from_rep = sender % n_rep

        @pl.when(jnp.logical_or(from_dom != dom, from_rep != rep))
        def _():
            pltpu.make_async_remote_copy(
                src_ref=send_bwd.at[0],
                dst_ref=returned.at[sender],
                send_sem=bwd_send.at[0],
                recv_sem=bwd_recv.at[sender],
                device_id=(from_dom, from_rep),
                device_id_type=MESH,
            ).wait_recv()

        return carry

    lax.fori_loop(0, n_dom, bwd_wait, 0, unroll=n_dom <= 16)

    out_ref[...] = dot_tn(returned[...].reshape(slots, feats), hot)

    def bwd_sent(step, carry):
        bwd_copy(step).wait_send()
        return carry

    lax.fori_loop(1, n_dom, bwd_sent, 0, unroll=n_dom <= 16)

    @pl.when(my_part != rep)
    def _():
        bwd_copy(0).wait_send()


def body(
    n_dom,
    n_rep,
    profiles,
    pack_index,
    obs_slot,
    interp_weight,
    departures,
    w_in,
    b_in,
    w_mid,
    b_mid,
    w_out,
):
    feats, width = profiles.shape
    cap = pack_index.shape[3]
    slots = n_dom * cap
    obs = obs_slot.shape[1]
    hidden = w_in.shape[1]
    vmem = pl.BlockSpec(memory_space=pltpu.VMEM)
    hbm = pl.BlockSpec(memory_space=pl.ANY)
    return pl.pallas_call(
        functools.partial(kernel, n_dom, n_rep),
        out_shape=jax.ShapeDtypeStruct((feats, width // n_rep), F32),
        in_specs=[vmem, vmem, vmem, vmem, hbm, hbm, vmem, hbm, vmem, hbm],
        out_specs=vmem,
        scratch_shapes=[
            pltpu.VMEM(departures.shape, F32),
            pltpu.VMEM(w_in.shape, BF16),
            pltpu.VMEM(w_mid.shape, BF16),
            pltpu.VMEM(w_out.shape, BF16),
            pltpu.VMEM((n_rep, n_dom // n_rep, cap, feats), BF16),
            pltpu.VMEM((n_dom, cap, feats), BF16),
            pltpu.VMEM((n_rep, n_dom, cap), jnp.int32),
            pltpu.VMEM((obs, 2 * slots), BF16),
            pltpu.VMEM((2, slots, obs), BF16),
            pltpu.VMEM((obs, hidden), F32),
            pltpu.VMEM((n_dom, cap, feats), BF16),
            pltpu.VMEM((n_dom, cap, feats), BF16),
            pltpu.SemaphoreType.DMA((4,)),
            pltpu.SemaphoreType.DMA((n_rep,)),
            pltpu.SemaphoreType.DMA((n_rep,)),
            pltpu.SemaphoreType.DMA((n_dom,)),
            pltpu.SemaphoreType.DMA((n_dom,)),
            pltpu.SemaphoreType.DMA((n_dom,)),
            pltpu.SemaphoreType.DMA((n_dom,)),
        ],
        compiler_params=pltpu.CompilerParams(
            collective_id=0, has_side_effects=True, vmem_limit_bytes=48 * 1024 * 1024
        ),
    )(
        profiles,
        pack_index.reshape(n_dom, cap),
        obs_slot,
        interp_weight,
        departures,
        w_in,
        b_in.reshape(1, hidden),
        w_mid,
        b_mid.reshape(1, hidden),
        w_out,
    )


def solution(mesh):
    placed = (
        P(None, "dom"),
        P("dom", "rep", None, None),
        P(None, ("dom", "rep")),
        P(None, ("dom", "rep")),
        P(None, ("dom", "rep")),
        P(),
        P(),
        P(),
        P(),
        P(),
    )
    return jax.shard_map(
        functools.partial(body, mesh.shape["dom"], mesh.shape["rep"]),
        mesh=mesh,
        in_specs=placed,
        out_specs=P(None, ("dom", "rep")),
        check_vma=False,
    )
```

time: 86.3 us -> 21.4 us (0.25); the launches traced: 84.8 us -> 21.2 us
  other arithmetic: 22.5 us -> 0 us
  starting transfers between devices: 19.8 us -> 0 us
  Pallas kernels: 0 us -> 16.2 us
  waiting for transfers between devices: 16 us -> 0 us
  local copies, waits for them, and re-layouts: 19.2 us -> 4.91 us
  matrix products: 6.99 us -> 0 us
    scatter-add x5 -> x0, other arithmetic: 21.6 us -> none  [the longest x4 20.2 us: spread_slots(): slot_adjoint.at[:, obs_slot[corner]].add(interp_weight[corner] * g_inputs)]
    all_to_all x4 -> x0, starting transfers between devices: 19.8 us -> none  [the longest x1 6.51 us: body(): lax.all_to_all(packed, 'dom', split_axis=1, concat_axis=1, tiled=True)]
    pallas_call x0 -> x1, Pallas kernels: none -> 16.2 us  [body(): pl.pallas_call(functools.partial(kernel, n_dom, n_rep), out_shape=jax.Sha...]
    all_to_all x4 -> x0, waiting for transfers between devices: 16 us -> none  [the longest x1 7.33 us: body(): lax.all_to_all(slot_adjoint, 'dom', split_axis=1, concat_axis=1, tiled=True)]
    gather x5 -> x0, local copies, waits for them, and re-layouts: 10.5 us -> none  [the longest x4 9.63 us: interpolate(): jnp.take(fetched, obs_slot[corner], axis=1).astype(jnp.float32)]
    dot_general x4 -> x0, matrix products: 6.99 us -> none  [the longest x2 3.72 us: contract_first(): lax.dot_general(matrix, values, (((0,), (0,)), ((), ())), preferred_eleme...]
    mul x4 -> x0, local copies, waits for them, and re-layouts: 1.94 us -> none  [spread_slots(): interp_weight[corner] * g_inputs]
    unnamed x23 -> x20, local copies, waits for them, and re-layouts: 3.61 us -> 4.91 us
  transfers between devices with their start and end apart: 4 -> 0, of which waited for: 3 -> 0; matrix products, arithmetic and copies ran while one was open for 46% -> 0% of each run, Pallas kernels for 0% -> 0%
where the time goes in v1:
time: 21.4 us; the launch traced here: 21.2 us
  Pallas kernels  16.2 us (76%)
  local copies, waits for them, and re-layouts  4.91 us (23%)
    pallas_call x1, Pallas kernels, body(): pl.pallas_call(functools.partial(kernel, n_dom, n_rep), out_shape=jax.Sha...  16.2 us
    unnamed x20, local copies, waits for them, and re-layouts  4.91 us

profile of v1, /device:TPU:1, one launch (start us, length us, event | category | flops | bytes accessed | tf_op | source)
XLA Modules:
  0.0 21.2 jit_solution(11800448131067285531)
XLA Ops:
  0.0 0.0 copy-start.3
  0.0 0.0 copy-start.4
  0.0 0.0 copy-start.5
  0.0 0.0 copy-start.6
  0.0 0.0 copy-start.7
  0.0 0.0 copy-start.8
  0.0 1.1 %copy.11.w_out_hbm = bf16[512,100]{1,0:T(8,128)(2,1)S(1)} copy(bf16[512,100]{0,1:T(8,128)(2,1)} %param.19) | data formatting | bytes 204800 | tf_op args[9]
  1.1 0.0 copy-done.3
  1.1 0.0 copy-done.4
  1.1 0.0 copy-done.5
  1.2 0.0 copy-done.6
  1.2 0.0 copy-done.7
  1.2 0.0 copy-done.8
  1.2 0.0 copy-start
  1.2 1.1 %copy-done = bf16[300,1024]{1,0:T(8,128)(2,1)S(1)} copy-done((bf16[300,1024]{1,0:T(8,128)(2,1)S(1)}, bf16[300,1024]{1,0:T(8,128)(2,1)}, u32[]{:S(2)}) %copy-start) | copy-done | bytes 614424
  2.3 0.0 copy-start.1
  2.3 1.0 %copy-done.1 = bf16[512,512]{1,0:T(8,128)(2,1)S(1)} copy-done((bf16[512,512]{1,0:T(8,128)(2,1)S(1)}, bf16[512,512]{1,0:T(8,128)(2,1)}, u32[]{:S(2)}) %copy-start.1) | copy-done | bytes 524312
  3.3 0.0 copy-start.2
  3.3 1.0 %copy-done.2 = bf16[300,512]{1,0:T(8,128)(2,1)S(1)} copy-done((bf16[300,512]{1,0:T(8,128)(2,1)S(1)}, bf16[300,512]{1,0:T(8,128)(2,1)}, u32[]{:S(2)}) %copy-start.2) | copy-done | bytes 307224
  4.3 16.2 %shard_map.100 = f32[300,256]{1,0:T(8,128)S(1)} custom-call(bf16[300,1024]{1,0:T(8,128)(2,1)S(1)} %copy-done, s32[8,16]{1,0:T(8,128)S(1)} %bitcast.3, s32[4,512]{1,0:T(4,128)S(1)} %copy-done.4, f32[4,512]{1,0:T(4,128)S(1)} %copy-done.5, f32[100,512]{1,0:T(8,128)S(1)} %copy-done.3, bf16[300,512]{1,0:T(8,128)(2,1)S(1)} %copy-done.2, f32[1,512]{1,0:T(1,128)S(1)} %bitcast.4, ...), custom_call_target="tpu_custom_call" | custom-call | tf_op jit(solution)/shard_map/pallas_call | solution.py:289
  20.4 0.7 %copy.13 = f32[300,256]{1,0:T(8,128)} copy(f32[300,256]{1,0:T(8,128)S(1)} %shard_map.100) | data formatting | bytes 614400
Async XLA Ops:
  0.0 1.1 %copy-start.3 = (f32[100,512]{1,0:T(8,128)S(1)}, f32[100,512]{1,0:T(8,128)}, u32[]{:S(2)}) copy-start(f32[100,512]{1,0:T(8,128)} %departures_hbm.1) | copy-start | bytes 614404
  0.0 1.1 %copy-start.4 = (s32[4,512]{1,0:T(4,128)S(1)}, s32[4,512]{1,0:T(4,128)}, u32[]{:S(2)}) copy-start(s32[4,512]{1,0:T(4,128)} %slot_ref.1) | copy-start | bytes 24580
  0.0 1.1 %copy-start.5 = (f32[4,512]{1,0:T(4,128)S(1)}, f32[4,512]{1,0:T(4,128)}, u32[]{:S(2)}) copy-start(f32[4,512]{1,0:T(4,128)} %weight_ref.1) | copy-start | bytes 24580
  0.0 1.1 %copy-start.6 = (s32[1,1,8,16]{3,2,1,0:T(8,128)S(1)}, s32[1,1,8,16]{3,2,1,0:T(8,128)}, u32[]{:S(2)}) copy-start(s32[1,1,8,16]{3,2,1,0:T(8,128)} %param.11) | copy-start | bytes 1540
  0.0 1.1 %copy-start.7 = (f32[512]{0:T(512)S(1)}, f32[512]{0:T(512)}, u32[]{:S(2)}) copy-start(f32[512]{0:T(512)} %param.16) | copy-start | bytes 6148
  0.0 1.1 %copy-start.8 = (f32[512]{0:T(512)S(1)}, f32[512]{0:T(512)}, u32[]{:S(2)}) copy-start(f32[512]{0:T(512)} %param.18) | copy-start | bytes 6148
  1.2 1.1 %copy-start = (bf16[300,1024]{1,0:T(8,128)(2,1)S(1)}, bf16[300,1024]{1,0:T(8,128)(2,1)}, u32[]{:S(2)}) copy-start(bf16[300,1024]{1,0:T(8,128)(2,1)} %profiles_ref.1) | copy-start | bytes 1843204
  2.3 1.0 %copy-start.1 = (bf16[512,512]{1,0:T(8,128)(2,1)S(1)}, bf16[512,512]{1,0:T(8,128)(2,1)}, u32[]{:S(2)}) copy-start(bf16[512,512]{1,0:T(8,128)(2,1)} %w_mid_hbm.1) | copy-start | bytes 1572868
  3.3 1.0 %copy-start.2 = (bf16[300,512]{1,0:T(8,128)(2,1)S(1)}, bf16[300,512]{1,0:T(8,128)(2,1)}, u32[]{:S(2)}) copy-start(bf16[300,512]{1,0:T(8,128)(2,1)} %w_in_hbm.1) | copy-start | bytes 921604

commit v2 on v1

--- a/solution.py
+++ b/solution.py
@@ -40,21 +40,27 @@
 def kernel(
     n_dom,
     n_rep,
+    profiles_hbm,
+    pack_hbm,
+    slot_hbm,
+    weight_hbm,
+    departures_hbm,
+    w_in_hbm,
+    b_in_hbm,
+    w_mid_hbm,
+    b_mid_hbm,
+    w_out_t_hbm,
+    out_ref,
     profiles_ref,
     pack_ref,
     slot_ref,
     weight_ref,
-    departures_hbm,
-    w_in_hbm,
-    b_in_ref,
-    w_mid_hbm,
-    b_mid_ref,
-    w_out_hbm,
-    out_ref,
     departures_ref,
     w_in_ref,
+    b_in_ref,
     w_mid_ref,
-    w_out_ref,
+    b_mid_ref,
+    w_out_t_ref,
     send_fwd,
     fetched,
     index_all,
@@ -80,6 +86,26 @@
     quarter = profiles_ref.shape[1] // n_rep
     my_part, my_group = dom % n_rep, dom // n_rep
 
+    loads = [
+        pltpu.make_async_copy(source, target, load_sem.at[k])
+        for k, (source, target) in enumerate(
+            (
+                (pack_hbm, pack_ref),
+                (profiles_hbm, profiles_ref),
+                (slot_hbm, slot_ref),
+                (weight_hbm, weight_ref),
+                (departures_hbm, departures_ref),
+                (w_out_t_hbm, w_out_t_ref),
+                (w_in_hbm, w_in_ref),
+                (b_in_hbm, b_in_ref),
+                (w_mid_hbm, w_mid_ref),
+                (b_mid_hbm, b_mid_ref),
+            )
+        )
+    ]
+    for load in loads:
+        load.start()
+
     barrier = pltpu.get_barrier_semaphore()
     for step in range(1, n_rep):
         pl.semaphore_signal(
@@ -94,20 +120,7 @@
 
     lax.fori_loop(1, n_dom, greet, 0, unroll=n_dom <= 16)
 
-    loads = [
-        pltpu.make_async_copy(source, target, load_sem.at[k])
-        for k, (source, target) in enumerate(
-            (
-                (departures_hbm, departures_ref),
-                (w_out_hbm, w_out_ref),
-                (w_in_hbm, w_in_ref),
-                (w_mid_hbm, w_mid_ref),
-            )
-        )
-    ]
-    for load in loads:
-        load.start()
-
+    loads[0].wait()
     seg = lax.broadcasted_iota(jnp.int32, (n_dom, cap), 0)
     local = pack_ref[...] - (seg % n_rep) * quarter
     index_all[rep] = local
@@ -116,6 +129,7 @@
     pick = (col == (row % per_rep) * n_rep + row // per_rep).astype(BF16)
     column = pick_column(pick, local.astype(BF16), cap).astype(jnp.int32)
     part_rows = per_rep * cap
+    loads[1].wait()
     for part in range(n_rep):
         hot = (
             column[part * part_rows : (part + 1) * part_rows]
@@ -159,6 +173,8 @@
 
     fetched[dom] = send_fwd[my_part, my_group]
 
+    loads[2].wait()
+    loads[3].wait()
     chunk = 128 if slots % 128 == 0 else slots
 
     def build(c, carry):
@@ -177,11 +193,11 @@
 
     lax.fori_loop(0, slots // chunk, build, 0, unroll=slots == chunk)
 
-    loads[0].wait()
-    loads[1].wait()
-    g_out[...] = dot_nt(departures_ref[...].T.astype(BF16), w_out_ref[...])
-    loads[2].wait()
-    loads[3].wait()
+    loads[4].wait()
+    loads[5].wait()
+    g_out[...] = dot_nn(departures_ref[...].T.astype(BF16), w_out_t_ref[...])
+    for load in loads[6:]:
+        load.wait()
 
     def fwd_wait(step, carry):
         fwd_copy(step).wait()
@@ -285,37 +301,7 @@
     obs = obs_slot.shape[1]
     hidden = w_in.shape[1]
     vmem = pl.BlockSpec(memory_space=pltpu.VMEM)
-    hbm = pl.BlockSpec(memory_space=pl.ANY)
-    return pl.pallas_call(
-        functools.partial(kernel, n_dom, n_rep),
-        out_shape=jax.ShapeDtypeStruct((feats, width // n_rep), F32),
-        in_specs=[vmem, vmem, vmem, vmem, hbm, hbm, vmem, hbm, vmem, hbm],
-        out_specs=vmem,
-        scratch_shapes=[
-            pltpu.VMEM(departures.shape, F32),
-            pltpu.VMEM(w_in.shape, BF16),
-            pltpu.VMEM(w_mid.shape, BF16),
-            pltpu.VMEM(w_out.shape, BF16),
-            pltpu.VMEM((n_rep, n_dom // n_rep, cap, feats), BF16),
-            pltpu.VMEM((n_dom, cap, feats), BF16),
-            pltpu.VMEM((n_rep, n_dom, cap), jnp.int32),
-            pltpu.VMEM((obs, 2 * slots), BF16),
-            pltpu.VMEM((2, slots, obs), BF16),
-            pltpu.VMEM((obs, hidden), F32),
-            pltpu.VMEM((n_dom, cap, feats), BF16),
-            pltpu.VMEM((n_dom, cap, feats), BF16),
-            pltpu.SemaphoreType.DMA((4,)),
-            pltpu.SemaphoreType.DMA((n_rep,)),
-            pltpu.SemaphoreType.DMA((n_rep,)),
-            pltpu.SemaphoreType.DMA((n_dom,)),
-            pltpu.SemaphoreType.DMA((n_dom,)),
-            pltpu.SemaphoreType.DMA((n_dom,)),
-            pltpu.SemaphoreType.DMA((n_dom,)),
-        ],
-        compiler_params=pltpu.CompilerParams(
-            collective_id=0, has_side_effects=True, vmem_limit_bytes=48 * 1024 * 1024
-        ),
-    )(
+    operands = (
         profiles,
         pack_index.reshape(n_dom, cap),
         obs_slot,
@@ -325,8 +311,35 @@
         b_in.reshape(1, hidden),
         w_mid,
         b_mid.reshape(1, hidden),
-        w_out,
+        w_out.T,
     )
+    return pl.pallas_call(
+        functools.partial(kernel, n_dom, n_rep),
+        out_shape=jax.ShapeDtypeStruct((feats, width // n_rep), F32),
+        in_specs=[pl.BlockSpec(memory_space=pltpu.HBM)] * len(operands),
+        out_specs=vmem,
+        scratch_shapes=[
+            *(pltpu.VMEM(operand.shape, operand.dtype) for operand in operands),
+            pltpu.VMEM((n_rep, n_dom // n_rep, cap, feats), BF16),
+            pltpu.VMEM((n_dom, cap, feats), BF16),
+            pltpu.VMEM((n_rep, n_dom, cap), jnp.int32),
+            pltpu.VMEM((obs, 2 * slots), BF16),
+            pltpu.VMEM((2, slots, obs), BF16),
+            pltpu.VMEM((obs, hidden), F32),
+            pltpu.VMEM((n_dom, cap, feats), BF16),
+            pltpu.VMEM((n_dom, cap, feats), BF16),
+            pltpu.SemaphoreType.DMA((len(operands),)),
+            pltpu.SemaphoreType.DMA((n_rep,)),
+            pltpu.SemaphoreType.DMA((n_rep,)),
+            pltpu.SemaphoreType.DMA((n_dom,)),
+            pltpu.SemaphoreType.DMA((n_dom,)),
+            pltpu.SemaphoreType.DMA((n_dom,)),
+            pltpu.SemaphoreType.DMA((n_dom,)),
+        ],
+        compiler_params=pltpu.CompilerParams(
+            collective_id=0, has_side_effects=True, vmem_limit_bytes=64 * 1024 * 1024
+        ),
+    )(*operands)
 
 
 def solution(mesh):

time: 21.4 us -> 18.8 us (0.88)
  local copies, waits for them, and re-layouts: 4.91 us -> 1.71 us
  Pallas kernels: 16.2 us -> 16.9 us
    unnamed x20 -> x1, local copies, waits for them, and re-layouts: 4.91 us -> 1.71 us
    pallas_call x1, Pallas kernels: 16.2 us -> 16.9 us  [body(): pl.pallas_call(functools.partial(kernel, n_dom, n_rep), out_shape=jax.Sha...]
where the time goes in v2:
time: 18.8 us; the launch traced here: 18.7 us
  Pallas kernels  16.9 us (90%)
  local copies, waits for them, and re-layouts  1.71 us (9%)
    pallas_call x1, Pallas kernels, body(): pl.pallas_call(functools.partial(kernel, n_dom, n_rep), out_shape=jax.Sha...  16.9 us
    unnamed x1, local copies, waits for them, and re-layouts  1.71 us

profile of v2, /device:TPU:1, one launch (start us, length us, event | category | flops | bytes accessed | tf_op | source)
XLA Modules:
  0.0 18.7 jit_solution(3264434569055819078)
XLA Ops:
  0.0 16.9 %shard_map.100 = f32[300,256]{1,0:T(8,128)} custom-call(bf16[300,1024]{1,0:T(8,128)(2,1)} %profiles_hbm.1, s32[8,16]{1,0:T(8,128)} %bitcast.5, s32[4,512]{1,0:T(4,128)} %slot_hbm.1, f32[4,512]{1,0:T(4,128)} %weight_hbm.1, f32[100,512]{1,0:T(8,128)} %departures_hbm.1, bf16[300,512]{1,0:T(8,128)(2,1)} %w_in_hbm.1, f32[1,512]{1,0:T(1,128)} %bitcast.6, ...), custom_call_target="tpu_custom_call" | custom-call | tf_op jit(solution)/shard_map/pallas_call | solution.py:316
  16.9 1.7 %copy.12 = f32[300,256]{1,0:T(8,128)} copy(f32[300,256]{1,0:T(8,128)} %shard_map.100) | data formatting | bytes 614400

commit v3 on v2

--- a/solution.py
+++ b/solution.py
@@ -35,6 +35,24 @@
     lane = lax.broadcasted_iota(jnp.int32, (rows, cap), 1)
     row = lax.broadcasted_iota(jnp.int32, (rows, cap), 0)
     return jnp.sum(jnp.where(lane == row % cap, spread, 0.0), axis=1, keepdims=True)
+
+
+def each(low, high, act):
+    if high - low <= 16:
+        for step in range(low, high):
+            act(step)
+    else:
+        lax.fori_loop(low, high, lambda step, carry: (act(step), carry)[1], 0)
+
+
+def partner(index, step, count):
+    if count > 16 or count & (count - 1):
+        return (index + step) % count
+    bits, result = (count - step) % count, index
+    for k in range(count.bit_length() - 1):
+        if (bits >> k) & 1:
+            result = result + (1 << k) * (1 - 2 * ((index // (1 << k)) % 2))
+    return result
 
 
 def kernel(
@@ -70,6 +88,7 @@
     send_bwd,
     returned,
     load_sem,
+    first_sem,
     idx_send,
     idx_recv,
     fwd_send,
@@ -86,12 +105,18 @@
     quarter = profiles_ref.shape[1] // n_rep
     my_part, my_group = dom % n_rep, dom // n_rep
 
+    first_loads = [pltpu.make_async_copy(pack_hbm, pack_ref, load_sem.at[0])] + [
+        pltpu.make_async_copy(
+            profiles_hbm.at[:, pl.ds(part * quarter, quarter)],
+            profiles_ref.at[:, pl.ds(part * quarter, quarter)],
+            first_sem.at[part],
+        )
+        for part in range(n_rep)
+    ]
     loads = [
-        pltpu.make_async_copy(source, target, load_sem.at[k])
+        pltpu.make_async_copy(source, target, load_sem.at[k + 1])
         for k, (source, target) in enumerate(
             (
-                (pack_hbm, pack_ref),
-                (profiles_hbm, profiles_ref),
                 (slot_hbm, slot_ref),
                 (weight_hbm, weight_ref),
                 (departures_hbm, departures_ref),
@@ -103,7 +128,7 @@
             )
         )
     ]
-    for load in loads:
+    for load in first_loads:
         load.start()
 
     barrier = pltpu.get_barrier_semaphore()
@@ -112,15 +137,17 @@
             barrier, inc=1, device_id=(dom, (rep + step) % n_rep), device_id_type=MESH
         )
 
-    def greet(step, carry):
+    def greet(step):
         pl.semaphore_signal(
-            barrier, inc=1, device_id=((dom + step) % n_dom, rep), device_id_type=MESH
-        )
-        return carry
-
-    lax.fori_loop(1, n_dom, greet, 0, unroll=n_dom <= 16)
-
-    loads[0].wait()
+            barrier, inc=1, device_id=(partner(dom, step, n_dom), rep), device_id_type=MESH
+        )
+
+    each(1, n_dom, greet)
+
+    for load in loads:
+        load.start()
+
+    first_loads[0].wait()
     seg = lax.broadcasted_iota(jnp.int32, (n_dom, cap), 0)
     local = pack_ref[...] - (seg % n_rep) * quarter
     index_all[rep] = local
@@ -129,19 +156,19 @@
     pick = (col == (row % per_rep) * n_rep + row // per_rep).astype(BF16)
     column = pick_column(pick, local.astype(BF16), cap).astype(jnp.int32)
     part_rows = per_rep * cap
-    loads[1].wait()
     for part in range(n_rep):
         hot = (
             column[part * part_rows : (part + 1) * part_rows]
             == lax.broadcasted_iota(jnp.int32, (part_rows, quarter), 1)
         ).astype(BF16)
+        first_loads[1 + part].wait()
         packed = dot_nt(hot, profiles_ref[:, part * quarter : (part + 1) * quarter])
         send_fwd[part] = packed.astype(BF16).reshape(per_rep, cap, feats)
 
     pl.semaphore_wait(barrier, n_dom + n_rep - 2)
 
     def fwd_copy(step):
-        peer = (dom + step) % n_dom
+        peer = partner(dom, step, n_dom)
         return pltpu.make_async_remote_copy(
             src_ref=send_fwd.at[peer % n_rep, peer // n_rep],
             dst_ref=fetched.at[dom],
@@ -151,11 +178,10 @@
             device_id_type=MESH,
         )
 
-    def fwd_start(step, carry):
+    def fwd_start(step):
         fwd_copy(step).start()
-        return carry
-
-    lax.fori_loop(1, n_dom, fwd_start, 0, unroll=n_dom <= 16)
+
+    each(1, n_dom, fwd_start)
 
     idx_copies = [
         pltpu.make_async_remote_copy(
@@ -173,8 +199,8 @@
 
     fetched[dom] = send_fwd[my_part, my_group]
 
-    loads[2].wait()
-    loads[3].wait()
+    loads[0].wait()
+    loads[1].wait()
     chunk = 128 if slots % 128 == 0 else slots
 
     def build(c, carry):
@@ -184,8 +210,8 @@
         for k in range(4):
             total = total + jnp.where(ids == slot_ref[k : k + 1, :], weight_ref[k : k + 1, :], 0.0)
         high, low = split_high_low(total)
-        spread_s[0, pl.ds(first, chunk), :] = high
-        spread_s[1, pl.ds(first, chunk), :] = low
+        spread_s[pl.ds(first, chunk), :] = high
+        spread_s[pl.ds(pl.multiple_of(slots + first, chunk), chunk), :] = low
         high_t, low_t = split_high_low(total.T)
         spread_t[:, pl.ds(first, chunk)] = high_t
         spread_t[:, pl.ds(pl.multiple_of(slots + first, chunk), chunk)] = low_t
@@ -193,17 +219,16 @@
 
     lax.fori_loop(0, slots // chunk, build, 0, unroll=slots == chunk)
 
-    loads[4].wait()
-    loads[5].wait()
+    loads[2].wait()
+    loads[3].wait()
     g_out[...] = dot_nn(departures_ref[...].T.astype(BF16), w_out_t_ref[...])
-    for load in loads[6:]:
+    for load in loads[4:]:
         load.wait()
 
-    def fwd_wait(step, carry):
-        fwd_copy(step).wait()
-        return carry
-
-    lax.fori_loop(1, n_dom, fwd_wait, 0, unroll=n_dom <= 16)
+    def fwd_wait(step):
+        fwd_copy(step).wait_recv()
+
+    each(1, n_dom, fwd_wait)
 
     columns = fetched[...].reshape(slots, feats)
     inputs = dot_nn(spread_t[...], jnp.concatenate([columns, columns], axis=0)).astype(BF16)
@@ -211,12 +236,13 @@
     act_two = jnp.tanh(dot_nn(act_one.astype(BF16), w_mid_ref[...]) + b_mid_ref[...])
     g_two = (g_out[...] * (1.0 - act_two * act_two)).astype(BF16)
     g_one = (dot_nt(g_two, w_mid_ref[...]) * (1.0 - act_one * act_one)).astype(BF16)
-    hidden = dot_nn(spread_s[0], g_one) + dot_nn(spread_s[1], g_one)
+    both = dot_nn(spread_s[...], g_one)
+    hidden = both[:slots] + both[slots:]
     slot_adjoint = dot_nt(hidden.astype(BF16), w_in_ref[...])
     send_bwd[...] = slot_adjoint.astype(BF16).reshape(n_dom, cap, feats)
 
     def bwd_copy(step):
-        owner = (dom + step) % n_dom
+        owner = partner(dom, step, n_dom)
         return pltpu.make_async_remote_copy(
             src_ref=send_bwd.at[owner],
             dst_ref=returned.at[my_group * n_rep + rep],
@@ -226,11 +252,10 @@
             device_id_type=MESH,
         )
 
-    def bwd_start(step, carry):
+    def bwd_start(step):
         bwd_copy(step).start()
-        return carry
-
-    lax.fori_loop(1, n_dom, bwd_start, 0, unroll=n_dom <= 16)
+
+    each(1, n_dom, bwd_start)
 
     @pl.when(my_part != rep)
     def _():
@@ -249,7 +274,7 @@
     target = pick_column(pick, table, cap).astype(jnp.int32)
     hot = (target == lax.broadcasted_iota(jnp.int32, (slots, quarter), 1)).astype(BF16)
 
-    def bwd_wait(sender, carry):
+    def bwd_wait(sender):
         from_dom = (sender // n_rep) * n_rep + rep
         from_rep = sender % n_rep
 
@@ -264,17 +289,16 @@
                 device_id_type=MESH,
             ).wait_recv()
 
-        return carry
-
-    lax.fori_loop(0, n_dom, bwd_wait, 0, unroll=n_dom <= 16)
+
+    each(0, n_dom, bwd_wait)
 
     out_ref[...] = dot_tn(returned[...].reshape(slots, feats), hot)
 
-    def bwd_sent(step, carry):
+    def bwd_sent(step):
         bwd_copy(step).wait_send()
-        return carry
-
-    lax.fori_loop(1, n_dom, bwd_sent, 0, unroll=n_dom <= 16)
+
+    each(1, n_dom, bwd_sent)
+    each(1, n_dom, lambda step: fwd_copy(step).wait_send())
 
     @pl.when(my_part != rep)
     def _():
@@ -315,7 +339,7 @@
     )
     return pl.pallas_call(
         functools.partial(kernel, n_dom, n_rep),
-        out_shape=jax.ShapeDtypeStruct((feats, width // n_rep), F32),
+        out_shape=pltpu.VMEM((feats, width // n_rep), F32),
         in_specs=[pl.BlockSpec(memory_space=pltpu.HBM)] * len(operands),
         out_specs=vmem,
         scratch_shapes=[
@@ -324,11 +348,12 @@
             pltpu.VMEM((n_dom, cap, feats), BF16),
             pltpu.VMEM((n_rep, n_dom, cap), jnp.int32),
             pltpu.VMEM((obs, 2 * slots), BF16),
-            pltpu.VMEM((2, slots, obs), BF16),
+            pltpu.VMEM((2 * slots, obs), BF16),
             pltpu.VMEM((obs, hidden), F32),
             pltpu.VMEM((n_dom, cap, feats), BF16),
             pltpu.VMEM((n_dom, cap, feats), BF16),
             pltpu.SemaphoreType.DMA((len(operands),)),
+            pltpu.SemaphoreType.DMA((n_rep,)),
             pltpu.SemaphoreType.DMA((n_rep,)),
             pltpu.SemaphoreType.DMA((n_rep,)),
             pltpu.SemaphoreType.DMA((n_dom,)),
@@ -337,9 +362,9 @@
             pltpu.SemaphoreType.DMA((n_dom,)),
         ],
         compiler_params=pltpu.CompilerParams(
-            collective_id=0, has_side_effects=True, vmem_limit_bytes=64 * 1024 * 1024
+            collective_id=0, has_side_effects=True, vmem_limit_bytes=62 * 1024 * 1024
         ),
-    )(*operands)
+    )(*(pltpu.with_memory_space_constraint(x, pltpu.HBM) for x in operands))
 
 
 def solution(mesh):

time: 18.8 us -> 17.2 us (0.915)
  local copies, waits for them, and re-layouts: 1.71 us -> 0.72 us
  Pallas kernels: 16.9 us -> 16.3 us
    unnamed x1, local copies, waits for them, and re-layouts: 1.71 us -> 0.72 us
    pallas_call x1, Pallas kernels: 16.9 us -> 16.3 us  [body(): pl.pallas_call(functools.partial(kernel, n_dom, n_rep), out_shape=pltpu.V...]
where the time goes in v3:
time: 17.2 us; the launch traced here: 17 us
  Pallas kernels  16.3 us (95%)
  local copies, waits for them, and re-layouts  0.72 us (4%)
    pallas_call x1, Pallas kernels, body(): pl.pallas_call(functools.partial(kernel, n_dom, n_rep), out_shape=pltpu.V...  16.3 us
    unnamed x1, local copies, waits for them, and re-layouts  0.72 us

profile of v3, /device:TPU:1, one launch (start us, length us, event | category | flops | bytes accessed | tf_op | source)
XLA Modules:
  0.0 17.0 jit_solution(1178795378898297786)
XLA Ops:
  0.0 16.3 %shard_map.100 = f32[300,256]{1,0:T(8,128)S(1)} custom-call(bf16[300,1024]{1,0:T(8,128)(2,1)} %profiles_hbm.1, s32[8,16]{1,0:T(8,128)} %bitcast.5, s32[4,512]{1,0:T(4,128)} %slot_hbm.1, f32[4,512]{1,0:T(4,128)} %weight_hbm.1, f32[100,512]{1,0:T(8,128)} %departures_hbm.1, bf16[300,512]{1,0:T(8,128)(2,1)} %w_in_hbm.1, f32[1,512]{1,0:T(1,128)} %bitcast.6, ...), custom_call_target="tpu_custom_call" | custom-call | tf_op jit(solution)/shard_map/pallas_call | solution.py:340
  16.3 0.7 %copy.12 = f32[300,256]{1,0:T(8,128)} copy(f32[300,256]{1,0:T(8,128)S(1)} %shard_map.100) | data formatting | bytes 614400
